TPU v7x, 256 devices: a whole 4x4x8 slice. The times are simulated.
256 devices in a mesh: row: 16 (over z, core), col: 16 (over x, y).
Axes of the slice: x: 4, y: 4, z: 8, core: 2. Of those that a mesh axis runs over, the one named last changes fastest.
Arguments:
- kernel: float32 [12288, 12288], P('row', 'col'), may hold values from 0 to 3.1, as said below
Outputs:
- factored: float32 [12288, 12288], P('row', 'col')
Inputs may be any that keep to these rules, and one draw needn't show every extreme that they name: kernel is the block-cyclic storage of a symmetric positive definite matrix whose least eigenvalue is 0.5 or more.
All inputs are finite; a program needn't handle non-finite values.
Results may differ from a plain program's by a relative error of at most 0.0003.
Values sent between devices are 32-bit elements; how exact they have to be, the bound alone decides.
A program may use at most 64 MiB of HBM per device.

v0:
```python
import jax
import jax.numpy as jnp
from jax import lax
from jax.sharding import PartitionSpec as P

NB = 256
SUBPANELS = 4


def broadcast(value, axis, source):
    kept = jnp.where(lax.axis_index(axis) == source, value, 0).astype(value.dtype)
    return lax.psum(kept, axis)


def lower_inverse(factor):
    ident = jnp.eye(factor.shape[0], dtype=jnp.float32)
    return jax.scipy.linalg.solve_triangular(factor, ident, lower=True)


def outer_product(left, right):
    return lax.dot_general(
        left,
        right,
        (((1,), (1,)), ((), ())),
        precision=lax.Precision.HIGHEST,
        preferred_element_type=jnp.float32,
    )


def body(kernel):
    width_sub = NB
    rows_total, cols_total = kernel.shape
    rows_blocks = rows_total // width_sub
    cols_blocks = cols_total // width_sub
    row_count = lax.axis_size("row")
    col_count = lax.axis_size("col")
    row_index = lax.axis_index("row")
    col_index = lax.axis_index("col")
    row_global = jnp.arange(rows_total, dtype=jnp.int32) // width_sub * row_count + row_index
    col_global = jnp.arange(cols_total, dtype=jnp.int32) // width_sub * col_count + col_index
    identity = jnp.eye(width_sub, dtype=jnp.float32)
    matrix = kernel
    for sub_step in range(SUBPANELS):
        factor_matrix = matrix
        owner_row = sub_step % row_count
        local_row = sub_step // row_count
        owner_col = sub_step % col_count
        local_col = sub_step // col_count
        column_slab = factor_matrix[:, local_col * width_sub : (local_col + 1) * width_sub]
        corner = column_slab[local_row * width_sub : (local_row + 1) * width_sub]
        diag = broadcast(corner, "row", owner_row)
        diag = jnp.where(col_index == owner_col, diag, identity)
        factor_factor = jnp.linalg.cholesky(diag)
        factor_solved = outer_product(column_slab, lower_inverse(factor_factor))
        stacked = jnp.tile(factor_factor, (rows_blocks, 1))
        position = row_global[:, None]
        panel = broadcast(
            jnp.where(
                position > sub_step, factor_solved, jnp.where(position == sub_step, stacked, 0.0)
            ),
            "col",
            owner_col,
        )
        pieces = []
        for local_blk in range(cols_blocks):
            global_blk = local_blk * col_count + col_index
            piece = lax.dynamic_slice_in_dim(
                panel, global_blk // row_count * width_sub, width_sub, 0
            )
            pieces.append(broadcast(piece, "row", global_blk % row_count))
        across = jnp.concatenate(pieces, axis=0)
        kept = jnp.where(col_index == owner_col, panel, column_slab)
        factor_matrix = factor_matrix.at[
            :, local_col * width_sub : (local_col + 1) * width_sub
        ].set(kept)
        matrix, panel, across = (factor_matrix, panel, across)
        region = (row_global[:, None] > sub_step) & (col_global[None, :] > sub_step)
        matrix = matrix - jnp.where(region, outer_product(panel, across), 0.0)
    corner_zero = (row_global[:, None] < SUBPANELS) & (col_global[None, :] >= SUBPANELS)
    return jnp.where(corner_zero, 0.0, matrix)


def solution(mesh):
    return jax.shard_map(
        body,
        mesh=mesh,
        in_specs=(P("row", "col"),),
        out_specs=P("row", "col"),
        check_vma=False,
    )
```

profile of v0, /device:TPU:36, one launch (start us, length us, event | category | flops | bytes accessed | tf_op | source)
XLA Modules:
  0.0 1586.3 jit_solution(16395808268641596586)
XLA Ops:
  9.4 108.6 %all-reduce.18.cloned.1.call-done = f32[256,256]{0,1:T(8,128)} async-done(((f32[256,256]{0,1:T(8,128)}), f32[256,256]{0,1:T(8,128)}) %all-reduce.18.cloned.1.call-update) | async-done | bytes 262160 | tf_op jit(solution)/shard_map/psum | solution.py:12
  118.3 11.7 cholesky.214
  130.1 9.8 custom-call.17
  140.4 11.7 cholesky.231
  158.8 19.7 %custom-call.18 = f32[2,128,128]{1,2,0:T(8,128)S(1)} custom-call(f32[2,128,128]{2,1,0:T(8,128)S(1)} %get-tuple-element.81), custom_call_target="InvertDiagBlocksLowerTriangular" | custom-call | tf_op jit(solution)/shard_map/jit(_solve_triangular)/triangular_solve | solution.py:17
  186.1 97.3 %all-reduce.20.cloned.1.call-done = f32[768,256]{0,1:T(8,128)} async-done(((f32[768,256]{0,1:T(8,128)}), f32[768,256]{0,1:T(8,128)}) %all-reduce.20.cloned.1.call-update) | async-done | bytes 786448 | tf_op jit(solution)/shard_map/psum | solution.py:12
  286.4 108.5 %all-reduce.40.cloned.1.call-done = (f32[256,256]{0,1:T(8,128)}, f32[256,256]{0,1:T(8,128)}, f32[256,256]{0,1:T(8,128)}) async-done(((f32[256,256]{0,1:T(8,128)}, f32[256,256]{0,1:T(8,128)}, f32[256,256]{0,1:T(8,128)}), (f32[256,256]{0,1:T(8,128)}, f32[256,256]{0,1:T(8,128)}, f32[256,256]{0,1:T(8,128)})) %all-reduce.40.cloned.1.call-update) | async-done | bytes 786448 | tf_op jit(solution)/shard_map/psum | solution.py:12
  400.9 108.8 %all-reduce.22.cloned.1.call-done = f32[256,256]{0,1:T(8,128)} async-done(((f32[256,256]{0,1:T(8,128)}), f32[256,256]{0,1:T(8,128)}) %all-reduce.22.cloned.1.call-update) | async-done | bytes 262160 | tf_op jit(solution)/shard_map/psum | solution.py:12
  509.9 11.7 cholesky.248
  521.7 9.8 custom-call.19
  531.9 11.7 cholesky.265
  547.0 4.4 while.13
  551.4 19.7 %custom-call.20 = f32[2,128,128]{1,2,0:T(8,128)S(1)} custom-call(f32[2,128,128]{2,1,0:T(8,128)S(1)} %get-tuple-element.82), custom_call_target="InvertDiagBlocksLowerTriangular" | custom-call | tf_op jit(solution)/shard_map/jit(_solve_triangular)/triangular_solve | solution.py:17
  578.0 98.0 %all-reduce.24.cloned.1.call-done = f32[768,256]{0,1:T(8,128)} async-done(((f32[768,256]{0,1:T(8,128)}), f32[768,256]{0,1:T(8,128)}) %all-reduce.24.cloned.1.call-update) | async-done | bytes 786448 | tf_op jit(solution)/shard_map/psum | solution.py:12
  679.0 108.5 %all-reduce.38.cloned.1.call-done = (f32[256,256]{0,1:T(8,128)}, f32[256,256]{0,1:T(8,128)}, f32[256,256]{0,1:T(8,128)}) async-done(((f32[256,256]{0,1:T(8,128)}, f32[256,256]{0,1:T(8,128)}, f32[256,256]{0,1:T(8,128)}), (f32[256,256]{0,1:T(8,128)}, f32[256,256]{0,1:T(8,128)}, f32[256,256]{0,1:T(8,128)})) %all-reduce.38.cloned.1.call-update) | async-done | bytes 786448 | tf_op jit(solution)/shard_map/psum | solution.py:12
  787.5 4.2 select_subtract_fusion.1
  792.7 108.9 %all-reduce.26.cloned.1.call-done = f32[256,256]{0,1:T(8,128)} async-done(((f32[256,256]{0,1:T(8,128)}), f32[256,256]{0,1:T(8,128)}) %all-reduce.26.cloned.1.call-update) | async-done | bytes 262160 | tf_op jit(solution)/shard_map/psum | solution.py:12
  901.8 11.7 cholesky.282
  913.6 9.8 custom-call.21
  923.9 11.7 cholesky.299
  943.0 19.7 %custom-call.22 = f32[2,128,128]{1,2,0:T(8,128)S(1)} custom-call(f32[2,128,128]{2,1,0:T(8,128)S(1)} %get-tuple-element.83), custom_call_target="InvertDiagBlocksLowerTriangular" | custom-call | tf_op jit(solution)/shard_map/jit(_solve_triangular)/triangular_solve | solution.py:17
  969.5 98.0 %all-reduce.28.cloned.1.call-done = f32[768,256]{0,1:T(8,128)} async-done(((f32[768,256]{0,1:T(8,128)}), f32[768,256]{0,1:T(8,128)}) %all-reduce.28.cloned.1.call-update) | async-done | bytes 786448 | tf_op jit(solution)/shard_map/psum | solution.py:12
  1070.5 108.5 %all-reduce.36.cloned.1.call-done = (f32[256,256]{0,1:T(8,128)}, f32[256,256]{0,1:T(8,128)}, f32[256,256]{0,1:T(8,128)}) async-done(((f32[256,256]{0,1:T(8,128)}, f32[256,256]{0,1:T(8,128)}, f32[256,256]{0,1:T(8,128)}), (f32[256,256]{0,1:T(8,128)}, f32[256,256]{0,1:T(8,128)}, f32[256,256]{0,1:T(8,128)})) %all-reduce.36.cloned.1.call-update) | async-done | bytes 786448 | tf_op jit(solution)/shard_map/psum | solution.py:12
  1185.0 108.8 %all-reduce.30.cloned.1.call-done = f32[256,256]{0,1:T(8,128)} async-done(((f32[256,256]{0,1:T(8,128)}), f32[256,256]{0,1:T(8,128)}) %all-reduce.30.cloned.1.call-update) | async-done | bytes 262160 | tf_op jit(solution)/shard_map/psum | solution.py:12
  1294.0 11.7 cholesky.316
  1305.8 9.8 custom-call.23
  1316.1 11.7 cholesky.333
  1331.2 4.4 while.15
  1335.6 19.7 %custom-call.24 = f32[2,128,128]{1,2,0:T(8,128)S(1)} custom-call(f32[2,128,128]{2,1,0:T(8,128)S(1)} %get-tuple-element.84), custom_call_target="InvertDiagBlocksLowerTriangular" | custom-call | tf_op jit(solution)/shard_map/jit(_solve_triangular)/triangular_solve | solution.py:17
  1361.4 98.0 %all-reduce.32.cloned.1.call-done = f32[768,256]{0,1:T(8,128)} async-done(((f32[768,256]{0,1:T(8,128)}), f32[768,256]{0,1:T(8,128)}) %all-reduce.32.cloned.1.call-update) | async-done | bytes 786448 | tf_op jit(solution)/shard_map/psum | solution.py:12
  1462.4 108.5 %all-reduce.34.cloned.1.call-done = (f32[256,256]{0,1:T(8,128)}, f32[256,256]{0,1:T(8,128)}, f32[256,256]{0,1:T(8,128)}) async-done(((f32[256,256]{0,1:T(8,128)}, f32[256,256]{0,1:T(8,128)}, f32[256,256]{0,1:T(8,128)}), (f32[256,256]{0,1:T(8,128)}, f32[256,256]{0,1:T(8,128)}, f32[256,256]{0,1:T(8,128)})) %all-reduce.34.cloned.1.call-update) | async-done | bytes 786448 | tf_op jit(solution)/shard_map/psum | solution.py:12
  1570.9 5.0 subtract_select_fusion
  (172 shorter events, 92.3 us)
Async XLA Ops:
  6.5 111.5 %all-reduce.18.cloned.1.call-start = ((), (), s32[]{:S(2)}) async-start(), calls=%async_computation | async-start | bytes 524288 | tf_op jit(solution)/shard_map/psum | solution.py:12
  9.3 274.0 %all-reduce.20.cloned.1.call-start = ((), (), s32[]{:S(2)}) async-start(), calls=%async_computation.1 | async-start | bytes 1572864 | tf_op jit(solution)/shard_map/psum | solution.py:12
  185.3 209.5 %all-reduce.40.cloned.1.call-start = ((), (), s32[]{:S(2)}) async-start(), calls=%async_computation.11 | async-start | bytes 1572864 | tf_op jit(solution)/shard_map/psum | solution.py:12
  283.3 2.2 copy-start.5
  285.5 224.2 %all-reduce.22.cloned.1.call-start = ((), (), s32[]{:S(2)}) async-start(), calls=%async_computation.2 | async-start | bytes 524288 | tf_op jit(solution)/shard_map/psum | solution.py:12
  398.4 1.4 copy-start
  400.5 275.4 %all-reduce.24.cloned.1.call-start = ((), (), s32[]{:S(2)}) async-start(), calls=%async_computation.3 | async-start | bytes 1572864 | tf_op jit(solution)/shard_map/psum | solution.py:12
  547.0 27.9 %copy-start.1 = (f32[768,768]{0,1:T(8,128)S(1)}, f32[768,768]{0,1:T(8,128)}, u32[]{:S(2)}) copy-start(f32[768,768]{0,1:T(8,128)} %copy-done) | copy-start | bytes 7077892
  577.9 209.6 %all-reduce.38.cloned.1.call-start = ((), (), s32[]{:S(2)}) async-start(), calls=%async_computation.10 | async-start | bytes 1572864 | tf_op jit(solution)/shard_map/psum | solution.py:12
  675.9 2.2 copy-start.7
  678.1 223.4 %all-reduce.26.cloned.1.call-start = ((), (), s32[]{:S(2)}) async-start(), calls=%async_computation.4 | async-start | bytes 524288 | tf_op jit(solution)/shard_map/psum | solution.py:12
  679.0 108.5 %copy-start.2 = (f32[768,768]{0,1:T(8,128)}, f32[768,768]{0,1:T(8,128)S(1)}, u32[]{:S(2)}) copy-start(f32[768,768]{0,1:T(8,128)S(1)} %fusion.6) | copy-start | bytes 7077892
  792.4 275.1 %all-reduce.28.cloned.1.call-start = ((), (), s32[]{:S(2)}) async-start(), calls=%async_computation.5 | async-start | bytes 1572864 | tf_op jit(solution)/shard_map/psum | solution.py:12
  969.5 209.5 %all-reduce.36.cloned.1.call-start = ((), (), s32[]{:S(2)}) async-start(), calls=%async_computation.9 | async-start | bytes 1572864 | tf_op jit(solution)/shard_map/psum | solution.py:12
  1067.5 2.2 copy-start.8
  1069.6 224.2 %all-reduce.30.cloned.1.call-start = ((), (), s32[]{:S(2)}) async-start(), calls=%async_computation.6 | async-start | bytes 524288 | tf_op jit(solution)/shard_map/psum | solution.py:12
  1182.6 1.4 copy-start.3
  1184.7 274.7 %all-reduce.32.cloned.1.call-start = ((), (), s32[]{:S(2)}) async-start(), calls=%async_computation.7 | async-start | bytes 1572864 | tf_op jit(solution)/shard_map/psum | solution.py:12
  1331.2 27.3 %copy-start.4 = (f32[768,768]{0,1:T(8,128)S(1)}, f32[768,768]{0,1:T(8,128)}, u32[]{:S(2)}) copy-start(f32[768,768]{0,1:T(8,128)} %copy-done.3) | copy-start | bytes 7077892
  1361.4 209.5 %all-reduce.34.cloned.1.call-start = ((), (), s32[]{:S(2)}) async-start(), calls=%async_computation.8 | async-start | bytes 1572864 | tf_op jit(solution)/shard_map/psum | solution.py:12
  1459.4 2.1 copy-start.6
Sparse Core Ops, SparseCore 0:
  9.7 108.3 all-reduce.17
  185.4 97.8 all-reduce.19
  285.9 108.9 all-reduce.39
  400.7 108.9 all-reduce.21
  578.0 97.8 all-reduce.23
  678.5 108.9 all-reduce.37
  792.6 108.9 all-reduce.25
  969.6 97.8 all-reduce.27
  1070.1 108.9 all-reduce.35
  1184.8 108.9 all-reduce.29
  1361.5 97.8 all-reduce.31
  1461.9 108.9 all-reduce.33
where the time goes:
time: 1600 us; the launch traced here: 1590 us
  waiting for transfers between devices  1260 us (79%)
  other arithmetic  235 us (15%)
  matrix products  36 us (2%)
  local copies, waits for them, and re-layouts  32.7 us (2%)
  between operations  19.7 us (1%)
    psum x12, waiting for transfers between devices, broadcast(): return lax.psum(kept, axis)  1260 us
    another operation x27, other arithmetic, body(): factor_factor = jnp.linalg.cholesky(diag)  138 us
    another operation x9, other arithmetic, lower_inverse(): return jax.scipy.linalg.solve_triangular(factor, ident, lower=True)  81.6 us
  transfers between devices with their start and end apart: 12, of which 12 were waited for; matrix products, arithmetic and copies ran while one was open for 0% of the time, Pallas kernels for 0%

commit v1 on v0

v1 whole, which is shorter than its diff:
```python
import functools

import jax
import jax.numpy as jnp
from jax import lax
from jax.experimental import pallas as pl
from jax.experimental.pallas import tpu as pltpu
from jax.sharding import PartitionSpec as P

NB = 256
SUBPANELS = 4
MESH = pl.DeviceIdType.MESH
F32 = jnp.float32
BF16 = jnp.bfloat16


def split3(x):
    high = x.astype(BF16)
    rest = x - high.astype(F32)
    middle = rest.astype(BF16)
    low = (rest - middle.astype(F32)).astype(BF16)
    return high, middle, low


def split2(x):
    high = x.astype(BF16)
    return high, (x - high.astype(F32)).astype(BF16)


def dot_nn(a, b):
    return lax.dot_general(a, b, (((1,), (0,)), ((), ())), preferred_element_type=F32)


def dot_nt(a, b):
    return lax.dot_general(a, b, (((1,), (1,)), ((), ())), preferred_element_type=F32)


def dot3(dot, a, b):
    return dot(a[0], b[0]) + (dot(a[0], b[1]) + dot(a[1], b[0]))


def tree_sum(terms):
    while len(terms) > 1:
        terms = [sum(terms[i + 1 : i + 2], terms[i]) for i in range(0, len(terms), 2)]
    return terms[0]


def eliminate(tiles, s, first, active, iota):
    quarter, lane = divmod(first, 128)

    def spread(x):
        return jnp.broadcast_to(x, (8, 128))

    column = {
        t: [spread(tiles[t][quarter][:, lane + k : lane + k + 1]) for k in range(8)]
        for t in range(s, 4)
    }
    e = [[spread(column[s][k][i : i + 1, :]) if k <= i else None for k in range(8)] for i in range(8)]
    low = [[None] * 8 for _ in range(8)]
    inv = [[None] * 8 for _ in range(8)]
    for j in range(8):
        root = lax.rsqrt(e[j][j])
        for i in range(j + 1, 8):
            low[i][j] = e[i][j] * root
        for i in range(j + 1, 8):
            for k in range(j + 1, i + 1):
                e[i][k] = e[i][k] - low[i][j] * low[k][j]
        inv[j][j] = root
        for k in range(j):
            total = low[j][k] * inv[k][k]
            for m in range(k + 1, j):
                total = total + low[j][m] * inv[m][k]
            inv[j][k] = -(root * total)
    columns = []
    for k in range(8):
        value = inv[7][k]
        for i in range(6, k - 1, -1):
            value = jnp.where(iota == i, inv[i][k], value)
        if k > 0:
            value = jnp.where(iota < k, 0.0, value)
        columns.append(value)
    done = {
        q: tree_sum([columns[k] * spread(tiles[s][q][k : k + 1, :]) for k in range(8)])
        for q in active
    }
    for t in range(s + 1, 4):
        factor = [tree_sum([column[t][m] * inv[k][m] for m in range(k + 1)]) for k in range(8)]
        for q in active:
            tiles[t][q] = tiles[t][q] - tree_sum(
                [factor[k] * spread(done[q][k : k + 1, :]) for k in range(8)]
            )
    tiles[s].update(done)


def factor_block(work):
    iota = lax.broadcasted_iota(jnp.int32, (8, 128), 0)
    for slab in range(8):
        first = 32 * slab
        active = [0, 1, 2] if slab < 4 else [1, 2, 3]
        tiles = [
            {q: work[first + 8 * t : first + 8 * t + 8, 128 * q : 128 * q + 128] for q in active}
            for t in range(4)
        ]
        for s in range(4):
            eliminate(tiles, s, first + 8 * s, active, iota)
        for t in range(4):
            for q in active:
                work[first + 8 * t : first + 8 * t + 8, 128 * q : 128 * q + 128] = tiles[t][q]
        if slab == 7:
            break
        left = 128 * active[0]
        top = jnp.concatenate(
            [jnp.concatenate([tiles[t][q] for q in active], axis=1) for t in range(4)], axis=0
        )
        high, middle, low = split3(top)
        right = jnp.concatenate([high, middle, high, middle, low, high], axis=0)
        across = top[:, : 256 - left].T
        high, middle, low = split3(across)
        down = jnp.concatenate([high, high, middle, middle, high, low], axis=1)
        for begin, end in ((first + 32, first + 64), (first + 64, 256)):
            if begin < end:
                work[begin:end, left : left + 384] = work[begin:end, left : left + 384] - dot_nn(
                    down[begin - left : end - left], right
                )


def solve_kernel(
    a_ref, corner_ref, rows_ref, cols_ref, o_ref,
    work, corner, inv2, low2, p2, v2, total,
):
    row, col = lax.axis_index("row"), lax.axis_index("col")
    iota_r = lax.broadcasted_iota(jnp.int32, (NB, NB), 0)
    iota_c = lax.broadcasted_iota(jnp.int32, (NB, NB), 1)
    eye = jnp.where(iota_r == iota_c, 1.0, 0.0).astype(F32)
    corner[...] = corner_ref[...]
    total[...] = a_ref[...]

    def store2(ref, index, value):
        high, low = split2(value)
        ref[index, 0] = high
        ref[index, 1] = low

    def load2(ref, index):
        return ref[index, 0], ref[index, 1]

    def step(k, _):
        work[:, 0:NB] = corner[k, k]
        work[:, NB : 2 * NB] = eye
        factor_block(work)
        inverse = jnp.where(iota_r >= iota_c, work[:, NB : 2 * NB], 0.0)
        store2(inv2, 0, inverse)
        inv = load2(inv2, 0)

        def below(i, _):
            store2(low2, i * SUBPANELS + k, dot3(dot_nt, split2(corner[i, k]), inv))
            return 0

        lax.fori_loop(k + 1, SUBPANELS, below, 0)

        def trail(i, _):
            def inner(j, _):
                corner[i, j] = corner[i, j] - dot3(
                    dot_nt, load2(low2, i * SUBPANELS + k), load2(low2, j * SUBPANELS + k)
                )
                return 0

            return lax.fori_loop(k + 1, i + 1, inner, 0)

        lax.fori_loop(k + 1, SUBPANELS, trail, 0)

        def rest(m, carry):
            across, down = carry
            low = load2(low2, k * SUBPANELS + m)
            return (
                across - dot3(dot_nt, load2(p2, m), low),
                down - dot3(dot_nn, low, load2(v2, m)),
            )

        across, down = lax.fori_loop(0, k, rest, (rows_ref[k], cols_ref[k]))
        p = dot3(dot_nt, split2(across), inv)
        store2(p2, k, p)
        store2(v2, k, dot3(dot_nn, inv, split2(down)))
        total[...] = total[...] - dot3(dot_nn, load2(p2, k), load2(v2, k))

        @pl.when(col == k)
        def _():
            o_ref[:, 0:NB] = p

        return 0

    lax.fori_loop(0, SUBPANELS, step, 0)
    top = row < SUBPANELS
    left = col < SUBPANELS
    o_ref[:, NB:] = total[:, NB:]

    @pl.when(jnp.logical_not(left))
    def _():
        o_ref[:, 0:NB] = total[:, 0:NB]

    @pl.when(top)
    def _():
        o_ref[0:NB, NB:] = jnp.zeros((NB, 2 * NB), F32)

    @pl.when(jnp.logical_and(top, col > row))
    def _():
        o_ref[0:NB, 0:NB] = jnp.zeros((NB, NB), F32)

    @pl.when(jnp.logical_and(top, col == row))
    def _():
        o_ref[0:NB, 0:NB] = jnp.where(iota_r >= iota_c, o_ref[0:NB, 0:NB], 0.0)


def solve(a, corner, rows, cols):
    size = a.shape[0]
    vmem = pl.BlockSpec(memory_space=pltpu.VMEM)
    return pl.pallas_call(
        solve_kernel,
        out_shape=jax.ShapeDtypeStruct(a.shape, F32),
        in_specs=[vmem] * 4,
        out_specs=vmem,
        scratch_shapes=[
            pltpu.VMEM((NB, 2 * NB), F32),
            pltpu.VMEM((SUBPANELS, SUBPANELS, NB, NB), F32),
            pltpu.VMEM((1, 2, NB, NB), BF16),
            pltpu.VMEM((SUBPANELS * SUBPANELS, 2, NB, NB), BF16),
            pltpu.VMEM((SUBPANELS, 2, size, NB), BF16),
            pltpu.VMEM((SUBPANELS, 2, NB, size), BF16),
            pltpu.VMEM(a.shape, F32),
        ],
        compiler_params=pltpu.CompilerParams(vmem_limit_bytes=52 << 20),
        name="factor_and_update",
    )(a, corner, rows, cols)


def gather_kernel(
    a_ref, corner, rows, cols,
    z_send, z_recv, pair_send, pair_recv, x_send, x_recv, x_next, y_send, y_recv, y_next,
    d_send, d_recv, local,
):
    row, col = lax.axis_index("row"), lax.axis_index("col")
    z, core = row // 2, row % 2
    x, y = col // 4, col % 4

    def at(zz, cc, xx, yy):
        return (zz * 2 + cc, xx * 4 + yy)

    def remote(src, dst, send, recv, where):
        return pltpu.make_async_remote_copy(
            src_ref=src, dst_ref=dst, send_sem=send, recv_sem=recv,
            device_id=where, device_id_type=MESH,
        )

    up, down = at((z + 1) % 8, core, x, y), at((z + 7) % 8, core, x, y)
    pair = at(z, 1 - core, x, y)
    east, west = at(z, core, (x + 1) % 4, y), at(z, core, (x + 3) % 4, y)
    north, south = at(z, core, x, (y + 1) % 4), at(z, core, x, (y + 3) % 4)

    barrier = pltpu.get_barrier_semaphore()
    peers = (up, down, pair, east, west, north, south)
    for peer in peers:
        pl.semaphore_signal(barrier, inc=1, device_id=peer, device_id_type=MESH)
    pl.semaphore_wait(barrier, len(peers))

    @pl.when(row < SUBPANELS)
    def _():
        copy = pltpu.make_async_copy(a_ref.at[0:NB, :], cols.at[row], local.at[0])
        copy.start()
        copy.wait()

    @pl.when(x == 0)
    def _():
        copy = pltpu.make_async_copy(a_ref.at[:, 0:NB], rows.at[y], local.at[1])
        copy.start()
        copy.wait()

    def col_piece(slab, block):
        return cols.at[slab, :, block * NB : (block + 1) * NB]

    def z_copy(item, where, direction):
        half, block = item % 2, item // 2
        piece = col_piece(2 * half + core, block)
        return remote(piece, piece, z_send.at[item, direction], z_recv.at[item], where)

    def pair_copy(item, which):
        half, block = item % 2, item // 2
        piece = col_piece(2 * half + which, block)
        return remote(piece, piece, pair_send.at[item], pair_recv.at[item], pair)

    def z_route(half):
        if half == 0:
            return z <= 3, jnp.logical_or(z == 0, z >= 6)
        return jnp.logical_and(z >= 1, z <= 3), jnp.logical_or(z <= 1, z >= 6)

    def z_step(item):
        half = item % 2
        own = z == half

        @pl.when(jnp.logical_not(own))
        def _():
            z_copy(item, up, 0).wait_recv()

        to_up, to_down = z_route(half)

        @pl.when(to_up)
        def _():
            z_copy(item, up, 0).start()

        @pl.when(to_down)
        def _():
            z_copy(item, down, 1).start()

        pair_copy(item, core).start()

    def z_finish(item):
        half = item % 2
        to_up, to_down = z_route(half)

        @pl.when(to_up)
        def _():
            z_copy(item, up, 0).wait_send()

        @pl.when(to_down)
        def _():
            z_copy(item, down, 1).wait_send()

        pair_copy(item, core).wait_send()
        pair_copy(item, 1 - core).wait_recv()

    def item_ref(item, source, part):
        if item < 2:
            ref = corner.at[2 * item + core, source]
            base = 0
        else:
            ref = rows.at[source]
            base = (item - 2) * NB
        if part is None:
            return ref.at[base : base + NB, :]
        return ref.at[base + part * 128 : base + part * 128 + 128, :]

    def wanted(item, source):
        if item >= 2:
            return source >= 0
        return 2 * item + core >= source

    def whole(item, where, slot, recv):
        ref = item_ref(item, y, None)
        return remote(ref, ref, x_send.at[item, slot], recv, where)

    def x_half(item, part, where):
        ref = item_ref(item, y, part)
        return remote(ref, ref, x_send.at[item, 0], x_next.at[item, part], where)

    def x_step(item):
        ok = wanted(item, y)
        if item < 2:
            @pl.when(x == 0)
            def _():
                copy = pltpu.make_async_copy(
                    cols.at[2 * item + core, :, 0:NB], corner.at[2 * item + core, y], local.at[0]
                )
                copy.start()
                copy.wait()

        @pl.when(jnp.logical_and(ok, x == 0))
        def _():
            whole(item, east, 0, x_recv.at[item]).start()
            whole(item, west, 1, x_recv.at[item]).start()

        @pl.when(jnp.logical_and(ok, x == 1))
        def _():
            whole(item, east, 0, x_recv.at[item]).wait_recv()
            x_half(item, 0, east).start()

        @pl.when(jnp.logical_and(ok, x == 3))
        def _():
            whole(item, east, 0, x_recv.at[item]).wait_recv()
            x_half(item, 1, west).start()

        @pl.when(jnp.logical_and(ok, x == 2))
        def _():
            x_half(item, 0, east).wait_recv()
            x_half(item, 1, east).wait_recv()

    def x_finish(item):
        ok = wanted(item, y)

        @pl.when(jnp.logical_and(ok, x == 0))
        def _():
            whole(item, east, 0, x_recv.at[item]).wait_send()
            whole(item, west, 1, x_recv.at[item]).wait_send()

        @pl.when(jnp.logical_and(ok, x == 1))
        def _():
            x_half(item, 0, east).wait_send()

        @pl.when(jnp.logical_and(ok, x == 3))
        def _():
            x_half(item, 1, west).wait_send()

    def y_whole(item, source, side):
        ref = item_ref(item, source, None)
        return remote(
            ref, ref, y_send.at[item, side], y_recv.at[item, side], north if side == 0 else south
        )

    def y_half(item, source, side):
        ref = item_ref(item, source, side)
        return remote(
            ref, ref, y_send.at[item, 2 + side], y_next.at[item, side], north if side == 0 else south
        )

    before, after, opposite = (y + 3) % 4, (y + 1) % 4, (y + 2) % 4

    def y_start(item):
        @pl.when(wanted(item, y))
        def _():
            y_whole(item, y, 0).start()
            y_whole(item, y, 1).start()

    def y_step(item):
        @pl.when(wanted(item, before))
        def _():
            y_whole(item, before, 0).wait_recv()
            y_half(item, before, 0).start()

        @pl.when(wanted(item, after))
        def _():
            y_whole(item, after, 1).wait_recv()
            y_half(item, after, 1).start()

    def y_finish(item):
        @pl.when(wanted(item, opposite))
        def _():
            y_half(item, opposite, 0).wait_recv()
            y_half(item, opposite, 1).wait_recv()

        @pl.when(wanted(item, y))
        def _():
            y_whole(item, y, 0).wait_send()
            y_whole(item, y, 1).wait_send()

        @pl.when(wanted(item, before))
        def _():
            y_half(item, before, 0).wait_send()

        @pl.when(wanted(item, after))
        def _():
            y_half(item, after, 1).wait_send()

    def corner_copy(item, source, which):
        ref = corner.at[2 * item + which, source]
        return remote(ref, ref, d_send.at[item, source], d_recv.at[item, source], pair)

    def corner_each(item, which, action):
        for source in range(4):
            @pl.when(2 * item + which >= source)
            def _():
                action(corner_copy(item, source, which))

    def corner_start(item):
        corner_each(item, core, lambda c: c.start())

    def corner_finish(item):
        corner_each(item, core, lambda c: c.wait_send())
        corner_each(item, 1 - core, lambda c: c.wait_recv())

    order = (0, 1, 2, 3, 4)
    z_step(0)
    z_step(1)
    for item in order:
        x_step(item)
        y_start(item)
        if item >= 1:
            y_step(item - 1)
            z_step(item + 1)
    y_step(4)
    for item in order:
        x_finish(item)
        y_finish(item)
        if item < 2:
            corner_start(item)
    for item in range(2):
        corner_finish(item)
    for item in range(6):
        z_finish(item)


def gather(a):
    size = a.shape[0]
    hbm = pl.BlockSpec(memory_space=pl.ANY)
    dma = pltpu.SemaphoreType.DMA
    return pl.pallas_call(
        gather_kernel,
        out_shape=[
            jax.ShapeDtypeStruct((SUBPANELS, SUBPANELS, NB, NB), F32),
            jax.ShapeDtypeStruct((SUBPANELS, size, NB), F32),
            jax.ShapeDtypeStruct((SUBPANELS, NB, size), F32),
        ],
        in_specs=[hbm],
        out_specs=[hbm] * 3,
        scratch_shapes=[
            dma((6, 2)), dma((6,)), dma((6,)), dma((6,)),
            dma((5, 2)), dma((5,)), dma((5, 2)),
            dma((5, 4)), dma((5, 2)), dma((5, 2)),
            dma((2, 4)), dma((2, 4)), dma((2,)),
        ],
        compiler_params=pltpu.CompilerParams(collective_id=0, has_side_effects=True),
        name="gather_panels",
    )(a)


def body(kernel):
    corner, rows, cols = gather(kernel)
    return solve(kernel, corner, rows, cols)


def solution(mesh):
    return jax.shard_map(
        body,
        mesh=mesh,
        in_specs=(P("row", "col"),),
        out_specs=P("row", "col"),
        check_vma=False,
    )
```

time: 1600 us -> 221 us (0.14)
  the two profiles are of different devices: /device:TPU:36 before, /device:TPU:132 now
where the time goes in v1:
time: 221 us
  Pallas kernels  221 us (100%)
    pallas_call x1, Pallas kernels, gather(): pl.pallas_call(gather_kernel, out_shape=[jax.ShapeDtypeStruct((SUBPANELS,...  156 us
    pallas_call x1, Pallas kernels, solve(): pl.pallas_call(solve_kernel, out_shape=jax.ShapeDtypeStruct(a.shape, F32)...  65.4 us

profile of v1, /device:TPU:132, one launch (start us, length us, event | category | flops | bytes accessed | tf_op | source)
XLA Modules:
  0.0 221.1 jit_solution(4286438478478747566)
XLA Ops:
  0.0 155.6 %gather_panels.1 = (f32[4,4,256,256]{3,2,1,0:T(8,128)}, f32[4,768,256]{2,1,0:T(8,128)}, f32[4,256,768]{2,1,0:T(8,128)}) custom-call(f32[768,768]{1,0:T(8,128)} %a_ref.3), custom_call_target="tpu_custom_call" | custom-call | tf_op jit(solution)/shard_map/gather_panels/pallas_call | solution.py:492
  155.7 65.4 %factor_and_update.1 = f32[768,768]{1,0:T(8,128)} custom-call(f32[768,768]{1,0:T(8,128)} %a_ref.3, f32[4,4,256,256]{3,2,1,0:T(8,128)} %get-tuple-element.8.corner_ref, f32[4,768,256]{2,1,0:T(8,128)} %get-tuple-element.9.rows_ref, f32[4,256,768]{2,1,0:T(8,128)} %get-tuple-element.10.cols_ref), custom_call_target="tpu_custom_call" | custom-call | tf_op jit(solution)/shard_map/factor_and_update/pallas_call | solution.py:216

commit v2 on v0

v2 whole, which is shorter than its diff:
```python
import functools

import jax
import jax.numpy as jnp
from jax import lax
from jax.experimental import pallas as pl
from jax.experimental.pallas import tpu as pltpu
from jax.sharding import PartitionSpec as P

NB = 256
SUBPANELS = 4
MESH = pl.DeviceIdType.MESH
F32 = jnp.float32
BF16 = jnp.bfloat16


def split3(x):
    high = x.astype(BF16)
    rest = x - high.astype(F32)
    middle = rest.astype(BF16)
    low = (rest - middle.astype(F32)).astype(BF16)
    return high, middle, low


def split2(x):
    high = x.astype(BF16)
    return high, (x - high.astype(F32)).astype(BF16)


def dot_nn(a, b):
    return lax.dot_general(a, b, (((1,), (0,)), ((), ())), preferred_element_type=F32)


def dot_nt(a, b):
    return lax.dot_general(a, b, (((1,), (1,)), ((), ())), preferred_element_type=F32)


def dot3(dot, a, b):
    return dot(a[0], b[0]) + (dot(a[0], b[1]) + dot(a[1], b[0]))


def tree_sum(terms):
    while len(terms) > 1:
        terms = [sum(terms[i + 1 : i + 2], terms[i]) for i in range(0, len(terms), 2)]
    return terms[0]


def eliminate(tiles, s, first, active, iota):
    quarter, lane = divmod(first, 128)

    def spread(x):
        return jnp.broadcast_to(x, (8, 128))

    column = {
        t: [spread(tiles[t][quarter][:, lane + k : lane + k + 1]) for k in range(8)]
        for t in range(s, 4)
    }
    e = [[spread(column[s][k][i : i + 1, :]) if k <= i else None for k in range(8)] for i in range(8)]
    low = [[None] * 8 for _ in range(8)]
    inv = [[None] * 8 for _ in range(8)]
    for j in range(8):
        root = lax.rsqrt(e[j][j])
        for i in range(j + 1, 8):
            low[i][j] = e[i][j] * root
        for i in range(j + 1, 8):
            for k in range(j + 1, i + 1):
                e[i][k] = e[i][k] - low[i][j] * low[k][j]
        inv[j][j] = root
        for k in range(j):
            total = low[j][k] * inv[k][k]
            for m in range(k + 1, j):
                total = total + low[j][m] * inv[m][k]
            inv[j][k] = -(root * total)
    columns = []
    for k in range(8):
        value = inv[7][k]
        for i in range(6, k - 1, -1):
            value = jnp.where(iota == i, inv[i][k], value)
        if k > 0:
            value = jnp.where(iota < k, 0.0, value)
        columns.append(value)
    done = {
        q: tree_sum([columns[k] * spread(tiles[s][q][k : k + 1, :]) for k in range(8)])
        for q in active
    }
    for t in range(s + 1, 4):
        factor = [tree_sum([column[t][m] * inv[k][m] for m in range(k + 1)]) for k in range(8)]
        for q in active:
            tiles[t][q] = tiles[t][q] - tree_sum(
                [factor[k] * spread(done[q][k : k + 1, :]) for k in range(8)]
            )
    tiles[s].update(done)


def factor_block(work):
    iota = lax.broadcasted_iota(jnp.int32, (8, 128), 0)
    for slab in range(8):
        first = 32 * slab
        active = [0, 1, 2] if slab < 4 else [1, 2, 3]
        tiles = [
            {q: work[first + 8 * t : first + 8 * t + 8, 128 * q : 128 * q + 128] for q in active}
            for t in range(4)
        ]
        for s in range(4):
            eliminate(tiles, s, first + 8 * s, active, iota)
        for t in range(4):
            for q in active:
                work[first + 8 * t : first + 8 * t + 8, 128 * q : 128 * q + 128] = tiles[t][q]
        if slab == 7:
            break
        left = 128 * active[0]
        top = jnp.concatenate(
            [jnp.concatenate([tiles[t][q] for q in active], axis=1) for t in range(4)], axis=0
        )
        high, middle, low = split3(top)
        right = jnp.concatenate([high, middle, high, middle, low, high], axis=0)
        across = top[:, : 256 - left].T
        high, middle, low = split3(across)
        down = jnp.concatenate([high, high, middle, middle, high, low], axis=1)
        for begin, end in ((first + 32, first + 64), (first + 64, 256)):
            if begin < end:
                work[begin:end, left : left + 384] = work[begin:end, left : left + 384] - dot_nn(
                    down[begin - left : end - left], right
                )


ROW_CHUNKS = 6
RING_CHUNKS = 8
RING_LAG = 3
RING_STEPS = RING_CHUNKS + 5 * RING_LAG + 1


def factor_kernel(
    a_ref, o_ref,
    rows, cols, low, corner, work, p2, v2, column,
    local, c_send, c_recv, x_send, x_recv, y_send, y_recv, z_send, z_extra, z_recv,
    q_send, q_recv, r_send, r_recv, s_send, s_recv, t_send, t_recv,
    u_send, u_recv, w_send, w_recv, e_send, e_recv,
):
    size = a_ref.shape[0]
    row, col = lax.axis_index("row"), lax.axis_index("col")
    z, core = row // 2, row % 2
    x, y = col // 4, col % 4
    both, either, no = jnp.logical_and, jnp.logical_or, jnp.logical_not
    is_root = both(row == 0, col == 0)
    is_spreader = both(row == 1, col == 0)
    root, spreader = (0, 0), (1, 0)

    def at(zz, cc, xx, yy):
        return (zz * 2 + cc, xx * 4 + yy)

    def ring(step):
        return at((z + step) % 8, core, x, y)

    def plane(dx, dy):
        return at(z, core, (x + dx) % 4, (y + dy) % 4)

    pair = at(z, 1 - core, x, y)

    def remote(ref, send, recv, where, src=None):
        return pltpu.make_async_remote_copy(
            src_ref=ref if src is None else src, dst_ref=ref, send_sem=send, recv_sem=recv,
            device_id=where, device_id_type=MESH,
        )

    barrier = pltpu.get_barrier_semaphore()
    offsets = [(dx, dy) for dx in range(4) for dy in range(4) if dx or dy]
    peers = [ring(step) for step in range(1, 8)] + [plane(*o) for o in offsets] + [pair]
    for peer in peers:
        pl.semaphore_signal(barrier, inc=1, device_id=peer, device_id_type=MESH)
    owners = [(i, j) for i in range(SUBPANELS) for j in range(i + 1) if i or j]
    owner = both(both(row < SUBPANELS, col <= row), no(is_root))

    @pl.when(owner)
    def _():
        pl.semaphore_signal(barrier, inc=1, device_id=root, device_id_type=MESH)

    @pl.when(is_root)
    def _():
        for peer in owners:
            pl.semaphore_signal(barrier, inc=1, device_id=peer, device_id_type=MESH)

    keep = pltpu.make_async_copy(a_ref, o_ref, local.at[0])
    keep.start()
    own_cols = pltpu.make_async_copy(a_ref.at[0:NB, :], cols.at[row % SUBPANELS], local.at[1])
    own_rows = pltpu.make_async_copy(a_ref.at[:, 0:NB], rows.at[y], local.at[2])
    own_corner = pltpu.make_async_copy(a_ref.at[0:NB, 0:NB], corner.at[0, 0], local.at[3])
    pl.when(row < SUBPANELS)(own_cols.start)
    pl.when(x == 0)(own_rows.start)
    pl.when(is_root)(own_corner.start)
    total = len(peers) + jnp.where(owner, 1, 0) + jnp.where(is_root, len(owners), 0)
    pl.semaphore_wait(barrier, total)

    def corner_copy(i, j):
        return remote(
            corner.at[i, j], c_send.at[0], c_recv.at[i * SUBPANELS + j], root,
            src=a_ref.at[0:NB, 0:NB],
        )

    for i, j in owners:
        pl.when(both(row == i, col == j))(corner_copy(i, j).start)
    pl.when(row < SUBPANELS)(own_cols.wait)
    pl.when(x == 0)(own_rows.wait)

    def row_ref(source, chunk):
        length = size // ROW_CHUNKS
        return rows.at[source, chunk * length : (chunk + 1) * length, :]

    def x_copy(chunk, d):
        return remote(row_ref(y, chunk), x_send.at[chunk, d - 1], x_recv.at[chunk], plane(d, 0))

    def y_copy(chunk, d):
        return remote(
            row_ref(y, chunk), y_send.at[chunk, d - 1], y_recv.at[chunk, d - 1], plane(0, d)
        )

    def y_arrival(chunk, d):
        return remote(
            row_ref((y + 4 - d) % 4, chunk), y_send.at[chunk, d - 1], y_recv.at[chunk, d - 1], pair
        )

    def ring_ref(u, way, chunk):
        length = NB // 2 // RING_CHUNKS
        begin = pl.multiple_of(way * (NB // 2) + chunk * length, length)
        return cols.at[2 * u + core, pl.ds(begin, length), :]

    def distance(u, way):
        return (z - u + 8) % 8 if way == 0 else (u - z + 8) % 8

    def ring_copy(u, way, chunk):
        step = 1 if way == 0 else 7
        if (u, way) == (1, 1):
            where = at(jnp.where(z == 1, 7, (z + 7) % 8), core, x, y)
        else:
            where = ring(step)
        return remote(
            ring_ref(u, way, chunk), z_send.at[u, way, chunk], z_recv.at[u, way, chunk], where
        )

    def ring_second(chunk):
        return remote(ring_ref(1, 1, chunk), z_extra.at[chunk], z_recv.at[1, 1, chunk], ring(7))

    def ring_passes(u, way):
        passes = distance(u, way) < 7
        return both(passes, z != 0) if (u, way) == (1, 1) else passes

    def each_chunk(action):
        def one(chunk, _):
            action(chunk)
            return 0

        lax.fori_loop(0, RING_CHUNKS, one, 0)

    def slab_copy(u, which):
        return remote(cols.at[2 * u + which], q_send.at[u], q_recv.at[u], pair)

    @pl.when(x == 0)
    def _():
        for chunk in range(ROW_CHUNKS):
            for d in range(1, 4):
                x_copy(chunk, d).start()
                y_copy(chunk, d).start()

    def ring_start(chunk):
        for u in range(2):
            @pl.when(z == u)
            def _():
                for way in range(2):
                    ring_copy(u, way, chunk).start()
                if u == 1:
                    ring_second(chunk).start()

    each_chunk(ring_start)

    def group(k, begin, length):
        return low.at[k, 0 : SUBPANELS - k, pl.ds(begin, length), :]

    def give(k):
        return remote(group(k, 0, NB), r_send.at[k], r_recv.at[k], spreader)

    def deal(k, dx, dy):
        piece = (4 * dy + dx) * 16
        return remote(
            group(k, piece, 16), s_send.at[k, 4 * dx + dy - 1], s_recv.at[k], (1, dx * 4 + dy)
        )

    mine = pl.multiple_of((4 * y + x) * 16, 16)

    def climb(k, step):
        return remote(group(k, mine, 16), t_send.at[k, step - 1], t_recv.at[k], ring(step))

    def spread_x(k, d):
        return remote(group(k, mine, 16), u_send.at[k, d - 1], u_recv.at[k, d - 1], plane(d, 0))

    def spread_x_arrival(k, d):
        begin = pl.multiple_of((4 * y + (x + 4 - d) % 4) * 16, 16)
        return remote(group(k, begin, 16), u_send.at[k, d - 1], u_recv.at[k, d - 1], pair)

    def spread_y(k, d):
        begin = pl.multiple_of(y * 64, 64)
        return remote(group(k, begin, 64), w_send.at[k, d - 1], w_recv.at[k, d - 1], plane(0, d))

    def spread_y_arrival(k, d):
        begin = pl.multiple_of((y + 4 - d) % 4 * 64, 64)
        return remote(group(k, begin, 64), w_send.at[k, d - 1], w_recv.at[k, d - 1], pair)

    def to_pair(k):
        return remote(group(k, 0, NB), e_send.at[k], e_recv.at[k], pair)

    def x_goes(d):
        return both(core == 1, no(both(both(z == 0, y == 0), (x + d) % 4 == 0)))

    def y_goes(d):
        return both(core == 1, no(both(both(z == 0, x == 0), (y + d) % 4 == 0)))

    takes = both(core == 1, no(is_spreader))

    def stage1(k):
        @pl.when(is_spreader)
        def _():
            give(k).wait_recv()
            for dx, dy in offsets:
                deal(k, dx, dy).start()

    def stage2(k):
        @pl.when(both(core == 1, z == 0))
        def _():
            @pl.when(no(is_spreader))
            def _():
                remote(group(k, mine, 16), r_send.at[k], s_recv.at[k], pair).wait_recv()

            for step in range(1, 8):
                climb(k, step).start()

    def stage3(k):
        @pl.when(both(core == 1, z != 0))
        def _():
            climb(k, 1).wait_recv()

        for d in range(1, 4):
            pl.when(x_goes(d))(spread_x(k, d).start)

    def stage4(k):
        @pl.when(takes)
        def _():
            for d in range(1, 4):
                spread_x_arrival(k, d).wait_recv()

        for d in range(1, 4):
            pl.when(y_goes(d))(spread_y(k, d).start)

    def stage5(k):
        @pl.when(takes)
        def _():
            for d in range(1, 4):
                spread_y_arrival(k, d).wait_recv()
            to_pair(k).start()

        @pl.when(both(core == 0, no(is_root)))
        def _():
            to_pair(k).wait_recv()

    def group_sent(k):
        pl.when(is_root)(give(k).wait_send)

        @pl.when(is_spreader)
        def _():
            for dx, dy in offsets:
                deal(k, dx, dy).wait_send()

        @pl.when(both(core == 1, z == 0))
        def _():
            for step in range(1, 8):
                climb(k, step).wait_send()

        for d in range(1, 4):
            pl.when(x_goes(d))(spread_x(k, d).wait_send)
            pl.when(y_goes(d))(spread_y(k, d).wait_send)
        pl.when(takes)(to_pair(k).wait_send)

    iota_r = lax.broadcasted_iota(jnp.int32, (NB, NB), 0)
    iota_c = lax.broadcasted_iota(jnp.int32, (NB, NB), 1)

    def ring_step(n):
        for u in range(2):
            for way in range(2):
                away = distance(u, way)
                chunk = n - RING_LAG * (away - 1)

                @pl.when(
                    both(both(away > 0, ring_passes(u, way)), both(chunk >= 0, chunk < RING_CHUNKS))
                )
                def _():
                    copy = ring_copy(u, way, chunk)
                    copy.wait_recv()
                    copy.start()

    def row_step(chunk):
        @pl.when(x != 0)
        def _():
            x_copy(chunk, 1).wait_recv()
            for d in range(1, 4):
                y_copy(chunk, d).start()

    def ring_finish():
        for u in range(2):
            for way in range(2):
                @pl.when(both(distance(u, way) > 0, no(ring_passes(u, way))))
                def _():
                    each_chunk(lambda chunk: ring_copy(u, way, chunk).wait_recv())

            slab_copy(u, core).start()

    def slabs_arrived():
        for chunk in range(ROW_CHUNKS):
            for d in range(1, 4):
                y_arrival(chunk, d).wait_recv()
        for u in range(2):
            slab_copy(u, 1 - core).wait_recv()
        keep.wait()

    def store2(ref, index, value):
        high, rest = split2(value)
        ref[index, 0] = high
        ref[index, 1] = rest

    def load2(ref, index):
        return ref[index, 0], ref[index, 1]

    def update(k):
        inv = split2(low[k, 0])
        across, down = rows[k], cols[k]

        def rest(m, carry):
            across, down = carry
            block = split2(low[m, k - m])
            return (
                across - dot3(dot_nt, load2(p2, m), block),
                down - dot3(dot_nn, block, load2(v2, m)),
            )

        across, down = lax.fori_loop(0, k, rest, (across, down))
        p = dot3(dot_nt, split2(across), inv)
        store2(p2, k, p)
        store2(v2, k, dot3(dot_nn, inv, split2(down)))
        o_ref[...] = o_ref[...] - dot3(dot_nn, load2(p2, k), load2(v2, k))

        @pl.when(col == k)
        def _():
            column[...] = p

    @pl.when(is_root)
    def _():
        own_corner.wait()
        eye = jnp.where(iota_r == iota_c, 1.0, 0.0).astype(F32)

        def step(k, _):
            work[:, 0:NB] = corner[k, k]
            work[:, NB : 2 * NB] = eye
            factor_block(work)
            inverse = jnp.where(iota_r >= iota_c, work[:, NB : 2 * NB], 0.0)
            low[k, 0] = inverse
            inv = split2(inverse)

            @pl.when(k == 0)
            def _():
                for i, j in owners:
                    corner_copy(i, j).wait_recv()

            def below(i, _):
                low[k, i - k] = dot3(dot_nt, split2(corner[i, k]), inv)
                return 0

            lax.fori_loop(k + 1, SUBPANELS, below, 0)
            for fixed in range(SUBPANELS):
                pl.when(k == fixed)(give(fixed).start)

            def trail(i, _):
                def inner(j, _):
                    corner[i, j] = corner[i, j] - dot3(
                        dot_nt, split2(low[k, i - k]), split2(low[k, j - k])
                    )
                    return 0

                return lax.fori_loop(k + 1, i + 1, inner, 0)

            return lax.fori_loop(k + 1, SUBPANELS, trail, 0)

        lax.fori_loop(0, SUBPANELS, step, 0)
        ring_finish()
        slabs_arrived()
        lax.fori_loop(0, SUBPANELS, lambda k, c: (update(k), c)[1], 0)

    @pl.when(no(is_root))
    def _():
        plan = {
            8: [(stage1, 0)], 13: [(stage2, 0)], 17: [(stage3, 0)], 18: [(stage1, 1)],
            20: [(stage4, 0)], 22: [(stage2, 1)], 23: [(stage5, 0)],
        }
        for chunk in range(ROW_CHUNKS):
            plan.setdefault(3 + 4 * chunk, []).append((row_step, chunk))

        def one(n, _):
            ring_step(n)
            for when, actions in plan.items():
                @pl.when(n == when)
                def _():
                    for action, argument in actions:
                        action(argument)

            return 0

        lax.fori_loop(0, RING_STEPS, one, 0)
        stage3(1)
        ring_finish()
        stage1(2)
        stage4(1)
        stage2(2)
        stage5(1)

        def duties():
            stage3(2)
            stage1(3)
            stage4(2)
            stage2(3)

        pl.when(is_spreader)(duties)
        slabs_arrived()

        def some(k, _):
            update(k)
            for fixed in range(SUBPANELS - 1):
                @pl.when(k == fixed)
                def _():
                    if fixed == 0:
                        pl.when(no(is_spreader))(duties)
                    if fixed == 1:
                        stage5(2)
                    if fixed == 2:
                        stage3(3)
                        stage4(3)
                        stage5(3)

            return 0

        lax.fori_loop(0, SUBPANELS, some, 0)

    top, left = row < SUBPANELS, col < SUBPANELS

    @pl.when(left)
    def _():
        o_ref[:, 0:NB] = column[...]

    @pl.when(top)
    def _():
        o_ref[0:NB, NB:] = jnp.zeros((NB, size - NB), F32)

    @pl.when(both(top, col > row))
    def _():
        o_ref[0:NB, 0:NB] = jnp.zeros((NB, NB), F32)

    @pl.when(both(top, col == row))
    def _():
        o_ref[0:NB, 0:NB] = jnp.where(iota_r >= iota_c, o_ref[0:NB, 0:NB], 0.0)

    pl.when(owner)(corner_copy(0, 0).wait_send)

    @pl.when(x == 0)
    def _():
        for chunk in range(ROW_CHUNKS):
            for d in range(1, 4):
                x_copy(chunk, d).wait_send()

    for chunk in range(ROW_CHUNKS):
        for d in range(1, 4):
            y_copy(chunk, d).wait_send()
    for u in range(2):
        for way in range(2):
            @pl.when(ring_passes(u, way))
            def _():
                each_chunk(lambda chunk: ring_copy(u, way, chunk).wait_send())

        slab_copy(u, core).wait_send()
    pl.when(z == 1)(lambda: each_chunk(lambda chunk: ring_second(chunk).wait_send()))
    for k in range(SUBPANELS):
        group_sent(k)


def body(a):
    size = a.shape[0]
    dma = pltpu.SemaphoreType.DMA
    vmem = pltpu.VMEM
    return pl.pallas_call(
        factor_kernel,
        out_shape=jax.ShapeDtypeStruct(a.shape, F32),
        in_specs=[pl.BlockSpec(memory_space=pl.ANY)],
        out_specs=pl.BlockSpec(memory_space=pltpu.VMEM),
        scratch_shapes=[
            vmem((SUBPANELS, size, NB), F32),
            vmem((SUBPANELS, NB, size), F32),
            vmem((SUBPANELS, SUBPANELS, NB, NB), F32),
            vmem((SUBPANELS, SUBPANELS, NB, NB), F32),
            vmem((NB, 2 * NB), F32),
            vmem((SUBPANELS, 2, size, NB), BF16),
            vmem((SUBPANELS, 2, NB, size), BF16),
            vmem((size, NB), F32),
            dma((4,)),
            dma((1,)), dma((16,)),
            dma((ROW_CHUNKS, 3)), dma((ROW_CHUNKS,)),
            dma((ROW_CHUNKS, 3)), dma((ROW_CHUNKS, 3)),
            dma((2, 2, RING_CHUNKS)), dma((RING_CHUNKS,)), dma((2, 2, RING_CHUNKS)),
            dma((2,)), dma((2,)),
            dma((4,)), dma((4,)),
            dma((4, 15)), dma((4,)),
            dma((4, 7)), dma((4,)),
            dma((4, 3)), dma((4, 3)),
            dma((4, 3)), dma((4, 3)),
            dma((4,)), dma((4,)),
        ],
        compiler_params=pltpu.CompilerParams(
            collective_id=0, has_side_effects=True, vmem_limit_bytes=56 << 20
        ),
        name="factor_corner_and_update",
    )(a)


def solution(mesh):
    return jax.shard_map(
        body,
        mesh=mesh,
        in_specs=(P("row", "col"),),
        out_specs=P("row", "col"),
        check_vma=False,
    )
```

time: 1600 us -> 109 us (0.07)
  waiting for transfers between devices: 1260 us -> 0 us
  other arithmetic: 235 us -> 0 us
  Pallas kernels: 0 us -> 105 us
  matrix products: 36 us -> 0 us
  local copies, waits for them, and re-layouts: 32.7 us -> 3.22 us
  between operations: 19.7 us -> 0.01 us
    psum x12 -> x0, waiting for transfers between devices: 1260 us -> none  [broadcast(): return lax.psum(kept, axis)]
    another operation x37 -> x0, other arithmetic: 220 us -> none  [the longest x27 138 us: body(): factor_factor = jnp.linalg.cholesky(diag)]
    pallas_call x0 -> x1, Pallas kernels: none -> 105 us  [body(): pl.pallas_call(factor_kernel, out_shape=jax.ShapeDtypeStruct(a.shape, F32...]
    dot_general x8 -> x0, matrix products: 28.1 us -> none  [outer_product(): lax.dot_general(left, right, (((1,), (1,)), ((), ())), precision=lax.Prec...]
    another operation x45 -> x0, local copies, waits for them, and re-layouts: 24.3 us -> none  [the longest x29 15.5 us: lower_inverse(): return jax.scipy.linalg.solve_triangular(factor, ident, lower=True)]
  transfers between devices with their start and end apart: 12 -> 0, of which waited for: 12 -> 0; matrix products, arithmetic and copies ran while one was open for 0% -> 0% of each run, Pallas kernels for 0% -> 0%
where the time goes in v2:
time: 109 us; the launch traced here: 108 us
  Pallas kernels  105 us (96%)
  local copies, waits for them, and re-layouts  3.22 us (3%)
    pallas_call x1, Pallas kernels, body(): pl.pallas_call(factor_kernel, out_shape=jax.ShapeDtypeStruct(a.shape, F32...  105 us
    unnamed x1, local copies, waits for them, and re-layouts  3.22 us

profile of v2, /device:TPU:36, one launch (start us, length us, event | category | flops | bytes accessed | tf_op | source)
XLA Modules:
  0.0 108.5 jit_solution(3281454231303394707)
XLA Ops:
  0.0 105.2 %factor_corner_and_update.1 = f32[768,768]{1,0:T(8,128)} custom-call(f32[768,768]{1,0:T(8,128)} %a_ref.1), custom_call_target="tpu_custom_call" | custom-call | tf_op jit(solution)/shard_map/factor_corner_and_update/pallas_call | solution.py:593
  105.2 3.2 %copy.3 = f32[768,768]{1,0:T(8,128)} copy(f32[768,768]{1,0:T(8,128)} %factor_corner_and_update.1) | data formatting | bytes 4718592

commit v3 on v2

--- a/solution.py
+++ b/solution.py
@@ -125,7 +125,7 @@
 
 
 ROW_CHUNKS = 6
-RING_CHUNKS = 8
+RING_CHUNKS = 16
 RING_LAG = 3
 RING_STEPS = RING_CHUNKS + 5 * RING_LAG + 1
 
@@ -133,7 +133,7 @@
 def factor_kernel(
     a_ref, o_ref,
     rows, cols, low, corner, work, p2, v2, column,
-    local, c_send, c_recv, x_send, x_recv, y_send, y_recv, z_send, z_extra, z_recv,
+    local, c_send, c_recv, x_send, x_recv, y_send, y_recv, y_next, z_send, z_extra, z_recv,
     q_send, q_recv, r_send, r_recv, s_send, s_recv, t_send, t_recv,
     u_send, u_recv, w_send, w_recv, e_send, e_recv,
 ):
@@ -206,18 +206,94 @@
         length = size // ROW_CHUNKS
         return rows.at[source, chunk * length : (chunk + 1) * length, :]
 
-    def x_copy(chunk, d):
-        return remote(row_ref(y, chunk), x_send.at[chunk, d - 1], x_recv.at[chunk], plane(d, 0))
-
-    def y_copy(chunk, d):
-        return remote(
-            row_ref(y, chunk), y_send.at[chunk, d - 1], y_recv.at[chunk, d - 1], plane(0, d)
-        )
-
-    def y_arrival(chunk, d):
-        return remote(
-            row_ref((y + 4 - d) % 4, chunk), y_send.at[chunk, d - 1], y_recv.at[chunk, d - 1], pair
-        )
+    def row_half(source, chunk, part):
+        length = size // ROW_CHUNKS // 2
+        begin = (2 * chunk + part) * length
+        return rows.at[source, begin : begin + length, :]
+
+    def x_copy(chunk, side):
+        return remote(
+            row_ref(y, chunk), x_send.at[chunk, side], x_recv.at[chunk, 0], plane(1 + 2 * side, 0)
+        )
+
+    def x_half(chunk, side):
+        return remote(
+            row_half(y, chunk, side), x_send.at[chunk, 0], x_recv.at[chunk, side],
+            plane(1 + 2 * side, 0),
+        )
+
+    beside_root = both(both(x == 0, z == 0), core == 0)
+    direct = both(beside_root, y % 2 == 1)
+    passing = no(both(beside_root, y % 2 == 0))
+
+    def y_copy(chunk, side):
+        return remote(
+            row_ref(y, chunk), y_send.at[chunk, side], y_recv.at[chunk, side],
+            plane(0, 1 + 2 * side),
+        )
+
+    def y_direct(chunk, source):
+        return remote(
+            row_ref(source, chunk), y_send.at[chunk, 4], y_next.at[chunk, 0], plane(0, 2)
+        )
+
+    def y_arrival(chunk, side):
+        return remote(
+            row_ref((y + 3 + 2 * side) % 4, chunk), y_send.at[chunk, side], y_recv.at[chunk, side],
+            pair,
+        )
+
+    def y_half(chunk, side, source):
+        return remote(
+            row_half(source, chunk, side), y_send.at[chunk, 2 + side], y_next.at[chunk, side],
+            plane(0, 1 + 2 * side),
+        )
+
+    def y_start(chunk):
+        for side in range(2):
+            y_copy(chunk, side).start()
+        pl.when(direct)(y_direct(chunk, y).start)
+
+    def row_step(chunk):
+        for side in range(2):
+            @pl.when(x == 1 + 2 * side)
+            def _():
+                x_copy(chunk, 0).wait_recv()
+                x_half(chunk, side).start()
+
+        @pl.when(x == 2)
+        def _():
+            for side in range(2):
+                x_half(chunk, side).wait_recv()
+
+        pl.when(x != 0)(lambda: y_start(chunk))
+
+    def row_pass(chunk):
+        for side in range(2):
+            y_arrival(chunk, side).wait_recv()
+
+            @pl.when(passing)
+            def _():
+                y_half(chunk, side, (y + 3 + 2 * side) % 4).start()
+
+    def row_last(chunk):
+        @pl.when(direct)
+        def _():
+            y_direct(chunk, (y + 2) % 4).wait_recv()
+
+        @pl.when(no(direct))
+        def _():
+            for side in range(2):
+                y_half(chunk, side, (y + 2) % 4).wait_recv()
+
+    def rows_sent():
+        for chunk in range(ROW_CHUNKS):
+            for side in range(2):
+                pl.when(x == 0)(x_copy(chunk, side).wait_send)
+                pl.when(x == 1 + 2 * side)(x_half(chunk, side).wait_send)
+                y_copy(chunk, side).wait_send()
+                pl.when(passing)(y_half(chunk, side, y).wait_send)
+            pl.when(direct)(y_direct(chunk, y).wait_send)
 
     def ring_ref(u, way, chunk):
         length = NB // 2 // RING_CHUNKS
@@ -257,9 +333,9 @@
     @pl.when(x == 0)
     def _():
         for chunk in range(ROW_CHUNKS):
-            for d in range(1, 4):
-                x_copy(chunk, d).start()
-                y_copy(chunk, d).start()
+            for side in range(2):
+                x_copy(chunk, side).start()
+            y_start(chunk)
 
     def ring_start(chunk):
         for u in range(2):
@@ -395,13 +471,6 @@
                     copy.wait_recv()
                     copy.start()
 
-    def row_step(chunk):
-        @pl.when(x != 0)
-        def _():
-            x_copy(chunk, 1).wait_recv()
-            for d in range(1, 4):
-                y_copy(chunk, d).start()
-
     def ring_finish():
         for u in range(2):
             for way in range(2):
@@ -413,41 +482,38 @@
 
     def slabs_arrived():
         for chunk in range(ROW_CHUNKS):
-            for d in range(1, 4):
-                y_arrival(chunk, d).wait_recv()
+            row_last(chunk)
         for u in range(2):
             slab_copy(u, 1 - core).wait_recv()
         keep.wait()
-
-    def store2(ref, index, value):
-        high, rest = split2(value)
-        ref[index, 0] = high
-        ref[index, 1] = rest
-
-    def load2(ref, index):
-        return ref[index, 0], ref[index, 1]
+        rows_sent()
+        for u in range(2):
+            for way in range(2):
+                @pl.when(ring_passes(u, way))
+                def _():
+                    each_chunk(lambda chunk: ring_copy(u, way, chunk).wait_send())
+
+            slab_copy(u, core).wait_send()
+        pl.when(z == 1)(lambda: each_chunk(lambda chunk: ring_second(chunk).wait_send()))
 
     def update(k):
         inv = split2(low[k, 0])
-        across, down = rows[k], cols[k]
-
-        def rest(m, carry):
-            across, down = carry
-            block = split2(low[m, k - m])
-            return (
-                across - dot3(dot_nt, load2(p2, m), block),
-                down - dot3(dot_nn, block, load2(v2, m)),
-            )
-
-        across, down = lax.fori_loop(0, k, rest, (across, down))
-        p = dot3(dot_nt, split2(across), inv)
-        store2(p2, k, p)
-        store2(v2, k, dot3(dot_nn, inv, split2(down)))
-        o_ref[...] = o_ref[...] - dot3(dot_nn, load2(p2, k), load2(v2, k))
+        p = dot3(dot_nt, split2(rows[k]), inv)
+        p2[0], p2[1] = split2(p)
+        v2[0], v2[1] = split2(dot3(dot_nn, inv, split2(cols[k])))
+        o_ref[...] = o_ref[...] - dot3(dot_nn, (p2[0], p2[1]), (v2[0], v2[1]))
 
         @pl.when(col == k)
         def _():
             column[...] = p
+
+        def rest(m, _):
+            block = split2(low[k, m - k])
+            rows[m] = rows[m] - dot3(dot_nt, (p2[0], p2[1]), block)
+            cols[m] = cols[m] - dot3(dot_nn, block, (v2[0], v2[1]))
+            return 0
+
+        lax.fori_loop(k + 1, SUBPANELS, rest, 0)
 
     @pl.when(is_root)
     def _():
@@ -488,17 +554,20 @@
 
         lax.fori_loop(0, SUBPANELS, step, 0)
         ring_finish()
+        for chunk in range(ROW_CHUNKS):
+            row_pass(chunk)
         slabs_arrived()
         lax.fori_loop(0, SUBPANELS, lambda k, c: (update(k), c)[1], 0)
 
     @pl.when(no(is_root))
     def _():
         plan = {
-            8: [(stage1, 0)], 13: [(stage2, 0)], 17: [(stage3, 0)], 18: [(stage1, 1)],
-            20: [(stage4, 0)], 22: [(stage2, 1)], 23: [(stage5, 0)],
+            10: [(stage1, 0)], 16: [(stage2, 0)], 19: [(stage1, 1)], 22: [(stage3, 0)],
+            26: [(stage2, 1), (stage4, 0)],
         }
         for chunk in range(ROW_CHUNKS):
-            plan.setdefault(3 + 4 * chunk, []).append((row_step, chunk))
+            plan.setdefault(5 + 3 * chunk, []).append((row_step, chunk))
+            plan.setdefault(8 + 4 * chunk, []).append((row_pass, chunk))
 
         def one(n, _):
             ring_step(n)
@@ -514,17 +583,10 @@
         stage3(1)
         ring_finish()
         stage1(2)
+        stage2(2)
+        stage5(0)
         stage4(1)
-        stage2(2)
-        stage5(1)
-
-        def duties():
-            stage3(2)
-            stage1(3)
-            stage4(2)
-            stage2(3)
-
-        pl.when(is_spreader)(duties)
+        pl.when(is_spreader)(lambda: (stage3(2), stage4(2), stage1(3), stage2(3)) and None)
         slabs_arrived()
 
         def some(k, _):
@@ -533,11 +595,13 @@
                 @pl.when(k == fixed)
                 def _():
                     if fixed == 0:
-                        pl.when(no(is_spreader))(duties)
+                        pl.when(no(is_spreader))(lambda: stage3(2))
+                        stage5(1)
+                        pl.when(no(is_spreader))(lambda: (stage4(2), stage2(3)) and None)
                     if fixed == 1:
                         stage5(2)
+                        stage3(3)
                     if fixed == 2:
-                        stage3(3)
                         stage4(3)
                         stage5(3)
 
@@ -565,23 +629,6 @@
 
     pl.when(owner)(corner_copy(0, 0).wait_send)
 
-    @pl.when(x == 0)
-    def _():
-        for chunk in range(ROW_CHUNKS):
-            for d in range(1, 4):
-                x_copy(chunk, d).wait_send()
-
-    for chunk in range(ROW_CHUNKS):
-        for d in range(1, 4):
-            y_copy(chunk, d).wait_send()
-    for u in range(2):
-        for way in range(2):
-            @pl.when(ring_passes(u, way))
-            def _():
-                each_chunk(lambda chunk: ring_copy(u, way, chunk).wait_send())
-
-        slab_copy(u, core).wait_send()
-    pl.when(z == 1)(lambda: each_chunk(lambda chunk: ring_second(chunk).wait_send()))
     for k in range(SUBPANELS):
         group_sent(k)
 
@@ -601,13 +648,13 @@
             vmem((SUBPANELS, SUBPANELS, NB, NB), F32),
             vmem((SUBPANELS, SUBPANELS, NB, NB), F32),
             vmem((NB, 2 * NB), F32),
-            vmem((SUBPANELS, 2, size, NB), BF16),
-            vmem((SUBPANELS, 2, NB, size), BF16),
+            vmem((2, size, NB), BF16),
+            vmem((2, NB, size), BF16),
             vmem((size, NB), F32),
             dma((4,)),
             dma((1,)), dma((16,)),
-            dma((ROW_CHUNKS, 3)), dma((ROW_CHUNKS,)),
-            dma((ROW_CHUNKS, 3)), dma((ROW_CHUNKS, 3)),
+            dma((ROW_CHUNKS, 2)), dma((ROW_CHUNKS, 2)),
+            dma((ROW_CHUNKS, 5)), dma((ROW_CHUNKS, 2)), dma((ROW_CHUNKS, 2)),
             dma((2, 2, RING_CHUNKS)), dma((RING_CHUNKS,)), dma((2, 2, RING_CHUNKS)),
             dma((2,)), dma((2,)),
             dma((4,)), dma((4,)),

time: 109 us -> 94.7 us (0.87)
  Pallas kernels: 105 us -> 90.1 us
    pallas_call x1, Pallas kernels: 105 us -> 90.1 us  [body(): pl.pallas_call(factor_kernel, out_shape=jax.ShapeDtypeStruct(a.shape, F32...]
where the time goes in v3:
time: 94.7 us; the launch traced here: 93.4 us
  Pallas kernels  90.1 us (95%)
  local copies, waits for them, and re-layouts  3.22 us (3%)
    pallas_call x1, Pallas kernels, body(): pl.pallas_call(factor_kernel, out_shape=jax.ShapeDtypeStruct(a.shape, F32...  90.1 us
    unnamed x1, local copies, waits for them, and re-layouts  3.22 us

profile of v3, /device:TPU:36, one launch (start us, length us, event | category | flops | bytes accessed | tf_op | source)
XLA Modules:
  0.0 93.4 jit_solution(16332850891601458922)
XLA Ops:
  0.0 90.1 %factor_corner_and_update.1 = f32[768,768]{1,0:T(8,128)} custom-call(f32[768,768]{1,0:T(8,128)} %a_ref.1), custom_call_target="tpu_custom_call" | custom-call | tf_op jit(solution)/shard_map/factor_corner_and_update/pallas_call | solution.py:640
  90.1 3.2 %copy.3 = f32[768,768]{1,0:T(8,128)} copy(f32[768,768]{1,0:T(8,128)} %factor_corner_and_update.1) | data formatting | bytes 4718592

commit v4 on v3

--- a/solution.py
+++ b/solution.py
@@ -127,7 +127,8 @@
 ROW_CHUNKS = 6
 RING_CHUNKS = 16
 RING_LAG = 3
-RING_STEPS = RING_CHUNKS + 5 * RING_LAG + 1
+AHEAD = 2
+RING_STEPS = max(RING_CHUNKS + 5 * RING_LAG, 9 + 4 * (ROW_CHUNKS - 1))
 
 
 def factor_kernel(
@@ -254,6 +255,9 @@
             y_copy(chunk, side).start()
         pl.when(direct)(y_direct(chunk, y).start)
 
+    def row_first(chunk):
+        pl.when(x == 0)(lambda: first_start(chunk))
+
     def row_step(chunk):
         for side in range(2):
             @pl.when(x == 1 + 2 * side)
@@ -330,23 +334,22 @@
     def slab_copy(u, which):
         return remote(cols.at[2 * u + which], q_send.at[u], q_recv.at[u], pair)
 
-    @pl.when(x == 0)
+    def first_start(chunk):
+        for side in range(2):
+            x_copy(chunk, side).start()
+        y_start(chunk)
+
+    def ring_source(u, chunk, action):
+        for way in range(2):
+            action(ring_copy(u, way, chunk))
+        if u == 1:
+            action(ring_second(chunk))
+
+    @pl.when(is_root)
     def _():
         for chunk in range(ROW_CHUNKS):
-            for side in range(2):
-                x_copy(chunk, side).start()
-            y_start(chunk)
-
-    def ring_start(chunk):
-        for u in range(2):
-            @pl.when(z == u)
-            def _():
-                for way in range(2):
-                    ring_copy(u, way, chunk).start()
-                if u == 1:
-                    ring_second(chunk).start()
-
-    each_chunk(ring_start)
+            first_start(chunk)
+        each_chunk(lambda chunk: ring_source(0, chunk, lambda copy: copy.start()))
 
     def group(k, begin, length):
         return low.at[k, 0 : SUBPANELS - k, pl.ds(begin, length), :]
@@ -458,6 +461,15 @@
     iota_c = lax.broadcasted_iota(jnp.int32, (NB, NB), 1)
 
     def ring_step(n):
+        for u in range(2):
+            @pl.when(both(z == u, n < RING_CHUNKS))
+            def _():
+                @pl.when(n >= AHEAD)
+                def _():
+                    ring_source(u, n - AHEAD, lambda copy: copy.wait_send())
+
+                ring_source(u, n, lambda copy: copy.start())
+
         for u in range(2):
             for way in range(2):
                 away = distance(u, way)
@@ -488,13 +500,18 @@
         keep.wait()
         rows_sent()
         for u in range(2):
-            for way in range(2):
-                @pl.when(ring_passes(u, way))
+            def left(chunk):
+                @pl.when(both(z == u, either(is_root, chunk >= RING_CHUNKS - AHEAD)))
                 def _():
-                    each_chunk(lambda chunk: ring_copy(u, way, chunk).wait_send())
-
+                    ring_source(u, chunk, lambda copy: copy.wait_send())
+
+                for way in range(2):
+                    @pl.when(both(z != u, ring_passes(u, way)))
+                    def _():
+                        ring_copy(u, way, chunk).wait_send()
+
+            each_chunk(left)
             slab_copy(u, core).wait_send()
-        pl.when(z == 1)(lambda: each_chunk(lambda chunk: ring_second(chunk).wait_send()))
 
     def update(k):
         inv = split2(low[k, 0])
@@ -566,6 +583,7 @@
             26: [(stage2, 1), (stage4, 0)],
         }
         for chunk in range(ROW_CHUNKS):
+            plan.setdefault(max(0, 3 * chunk - 3), []).append((row_first, chunk))
             plan.setdefault(5 + 3 * chunk, []).append((row_step, chunk))
             plan.setdefault(8 + 4 * chunk, []).append((row_pass, chunk))
 
@@ -586,7 +604,10 @@
         stage2(2)
         stage5(0)
         stage4(1)
-        pl.when(is_spreader)(lambda: (stage3(2), stage4(2), stage1(3), stage2(3)) and None)
+        stage3(2)
+        pl.when(is_spreader)(
+            lambda: (stage4(2), stage1(3), stage2(3), stage3(3), stage4(3)) and None
+        )
         slabs_arrived()
 
         def some(k, _):
@@ -595,14 +616,13 @@
                 @pl.when(k == fixed)
                 def _():
                     if fixed == 0:
-                        pl.when(no(is_spreader))(lambda: stage3(2))
                         stage5(1)
                         pl.when(no(is_spreader))(lambda: (stage4(2), stage2(3)) and None)
                     if fixed == 1:
+                        pl.when(no(is_spreader))(lambda: stage3(3))
                         stage5(2)
-                        stage3(3)
                     if fixed == 2:
-                        stage4(3)
+                        pl.when(no(is_spreader))(lambda: stage4(3))
                         stage5(3)
 
             return 0

time: 94.7 us -> 88.3 us (0.932); the launches traced: 93.4 us -> 88.2 us
  Pallas kernels: 90.1 us -> 84.9 us
    pallas_call x1, Pallas kernels: 90.1 us -> 84.9 us  [body(): pl.pallas_call(factor_kernel, out_shape=jax.ShapeDtypeStruct(a.shape, F32...]
where the time goes in v4:
time: 88.3 us; the launch traced here: 88.2 us
  Pallas kernels  84.9 us (96%)
  local copies, waits for them, and re-layouts  3.22 us (4%)
    pallas_call x1, Pallas kernels, body(): pl.pallas_call(factor_kernel, out_shape=jax.ShapeDtypeStruct(a.shape, F32...  84.9 us
    unnamed x1, local copies, waits for them, and re-layouts  3.22 us

profile of v4, /device:TPU:36, one launch (start us, length us, event | category | flops | bytes accessed | tf_op | source)
XLA Modules:
  0.0 88.2 jit_solution(2359612244895787924)
XLA Ops:
  0.0 84.9 %factor_corner_and_update.1 = f32[768,768]{1,0:T(8,128)} custom-call(f32[768,768]{1,0:T(8,128)} %a_ref.1), custom_call_target="tpu_custom_call" | custom-call | tf_op jit(solution)/shard_map/factor_corner_and_update/pallas_call | solution.py:660
  84.9 3.2 %copy.3 = f32[768,768]{1,0:T(8,128)} copy(f32[768,768]{1,0:T(8,128)} %factor_corner_and_update.1) | data formatting | bytes 4718592

commit v5 on v4

--- a/solution.py
+++ b/solution.py
@@ -513,21 +513,28 @@
             each_chunk(left)
             slab_copy(u, core).wait_send()
 
+    def left3(x, axis):
+        high, rest = split2(x)
+        return jnp.concatenate([high, high, rest], axis=axis)
+
+    def right3(x, axis):
+        high, rest = split2(x)
+        return jnp.concatenate([high, rest, high], axis=axis)
+
     def update(k):
-        inv = split2(low[k, 0])
-        p = dot3(dot_nt, split2(rows[k]), inv)
-        p2[0], p2[1] = split2(p)
-        v2[0], v2[1] = split2(dot3(dot_nn, inv, split2(cols[k])))
-        o_ref[...] = o_ref[...] - dot3(dot_nn, (p2[0], p2[1]), (v2[0], v2[1]))
+        p = dot_nt(left3(rows[k], 1), right3(low[k, 0], 1))
+        p2[...] = left3(p, 1)
+        v2[...] = right3(dot_nn(left3(low[k, 0], 1), right3(cols[k], 0)), 0)
+        o_ref[...] = o_ref[...] - dot_nn(p2[...], v2[...])
 
         @pl.when(col == k)
         def _():
             column[...] = p
 
         def rest(m, _):
-            block = split2(low[k, m - k])
-            rows[m] = rows[m] - dot3(dot_nt, (p2[0], p2[1]), block)
-            cols[m] = cols[m] - dot3(dot_nn, block, (v2[0], v2[1]))
+            block = low[k, m - k]
+            rows[m] = rows[m] - dot_nt(p2[...], right3(block, 1))
+            cols[m] = cols[m] - dot_nn(left3(block, 1), v2[...])
             return 0
 
         lax.fori_loop(k + 1, SUBPANELS, rest, 0)
@@ -668,8 +675,8 @@
             vmem((SUBPANELS, SUBPANELS, NB, NB), F32),
             vmem((SUBPANELS, SUBPANELS, NB, NB), F32),
             vmem((NB, 2 * NB), F32),
-            vmem((2, size, NB), BF16),
-            vmem((2, NB, size), BF16),
+            vmem((size, 3 * NB), BF16),
+            vmem((3 * NB, size), BF16),
             vmem((size, NB), F32),
             dma((4,)),
             dma((1,)), dma((16,)),

time: 88.3 us -> 88 us (level)
  no operation moved by 1% of the time
where the time goes in v5:
time: 88 us; the launch traced here: 87.9 us
  Pallas kernels  84.7 us (96%)
  local copies, waits for them, and re-layouts  3.22 us (4%)
    pallas_call x1, Pallas kernels, body(): pl.pallas_call(factor_kernel, out_shape=jax.ShapeDtypeStruct(a.shape, F32...  84.7 us
    unnamed x1, local copies, waits for them, and re-layouts  3.22 us

profile of v5, /device:TPU:36, one launch (start us, length us, event | category | flops | bytes accessed | tf_op | source)
XLA Modules:
  0.0 87.9 jit_solution(3116088492557035095)
XLA Ops:
  0.0 84.7 %factor_corner_and_update.1 = f32[768,768]{1,0:T(8,128)} custom-call(f32[768,768]{1,0:T(8,128)} %a_ref.1), custom_call_target="tpu_custom_call" | custom-call | tf_op jit(solution)/shard_map/factor_corner_and_update/pallas_call | solution.py:667
  84.7 3.2 %copy.3 = f32[768,768]{1,0:T(8,128)} copy(f32[768,768]{1,0:T(8,128)} %factor_corner_and_update.1) | data formatting | bytes 4718592

commit v6 on v5

--- a/solution.py
+++ b/solution.py
@@ -550,7 +550,7 @@
             factor_block(work)
             inverse = jnp.where(iota_r >= iota_c, work[:, NB : 2 * NB], 0.0)
             low[k, 0] = inverse
-            inv = split2(inverse)
+            inv = right3(inverse, 1)
 
             @pl.when(k == 0)
             def _():
@@ -558,7 +558,7 @@
                     corner_copy(i, j).wait_recv()
 
             def below(i, _):
-                low[k, i - k] = dot3(dot_nt, split2(corner[i, k]), inv)
+                low[k, i - k] = dot_nt(left3(corner[i, k], 1), inv)
                 return 0
 
             lax.fori_loop(k + 1, SUBPANELS, below, 0)
@@ -567,8 +567,8 @@
 
             def trail(i, _):
                 def inner(j, _):
-                    corner[i, j] = corner[i, j] - dot3(
-                        dot_nt, split2(low[k, i - k]), split2(low[k, j - k])
+                    corner[i, j] = corner[i, j] - dot_nt(
+                        left3(low[k, i - k], 1), right3(low[k, j - k], 1)
                     )
                     return 0
 

time: 88 us -> 88 us (level)
  no operation moved by 1% of the time
where the time goes in v6:
time: 88 us; the launch traced here: 87.9 us
  Pallas kernels  84.7 us (96%)
  local copies, waits for them, and re-layouts  3.22 us (4%)
    pallas_call x1, Pallas kernels, body(): pl.pallas_call(factor_kernel, out_shape=jax.ShapeDtypeStruct(a.shape, F32...  84.7 us
    unnamed x1, local copies, waits for them, and re-layouts  3.22 us

profile of v6, /device:TPU:36, one launch (start us, length us, event | category | flops | bytes accessed | tf_op | source)
XLA Modules:
  0.0 87.9 jit_solution(2099873335074096021)
XLA Ops:
  0.0 84.7 %factor_corner_and_update.1 = f32[768,768]{1,0:T(8,128)} custom-call(f32[768,768]{1,0:T(8,128)} %a_ref.1), custom_call_target="tpu_custom_call" | custom-call | tf_op jit(solution)/shard_map/factor_corner_and_update/pallas_call | solution.py:667
  84.7 3.2 %copy.3 = f32[768,768]{1,0:T(8,128)} copy(f32[768,768]{1,0:T(8,128)} %factor_corner_and_update.1) | data formatting | bytes 4718592
